TPU v7x, 32 devices: a whole 2x2x4 slice. The times are simulated.
32 devices in a mesh: dp: 8 (over y, x, core), tensor: 4 (over z).
Axes of the slice: x: 2, y: 2, z: 4, core: 2. Of those that a mesh axis runs over, the one named last changes fastest.
Arguments:
- hidden_in: bfloat16 [32768, 1024], P(('dp', 'tensor')), may hold values from -6 to 6
- norm_gain: float32 [1024], replicated, may hold values from 0.5 to 1.5
- w_zx: bfloat16 [1024, 2, 2048], P(None, None, 'tensor'), may hold values from -0.1875 to 0.1875
- w_dt: bfloat16 [1024, 32], P(None, 'tensor'), may hold values from -0.1875 to 0.1875
- w_bc: bfloat16 [1024, 256], replicated, may hold values from -0.1875 to 0.1875
- conv_x: float32 [4, 2048], P(None, 'tensor'), may hold values from -3 to 3
- conv_x_bias: float32 [2048], P('tensor'), may hold values from -3 to 3
- conv_bc: float32 [4, 256], replicated, may hold values from -3 to 3
- conv_bc_bias: float32 [256], replicated, may hold values from -3 to 3
- a_log: float32 [32], P('tensor'), may hold values from 0 to 2.77
- dt_bias: float32 [32], P('tensor'), may hold values from -4.6 to -1
- d_skip: float32 [32], P('tensor'), may hold values from 0.5 to 1.5
- gate_gain: float32 [2048], P('tensor'), may hold values from 0.5 to 1.5
- w_out: bfloat16 [2048, 1024], P('tensor'), may hold values from -0.125 to 0.125
- cotangent: bfloat16 [32768, 1024], P(('dp', 'tensor')), may hold values from -6 to 6
Outputs:
- output: bfloat16 [32768, 1024], P(('dp', 'tensor'))
- input_grad: bfloat16 [32768, 1024], P(('dp', 'tensor'))
- grad_norm_gain: float32 [1024], replicated
- grad_w_zx: float32 [1024, 2, 2048], P('dp', None, 'tensor')
- grad_w_dt: float32 [1024, 32], P('dp', 'tensor')
- grad_w_bc: float32 [1024, 256], P('dp')
- grad_conv_x: float32 [4, 2048], P(None, 'tensor')
- grad_conv_x_bias: float32 [2048], P('tensor')
- grad_conv_bc: float32 [4, 256], replicated
- grad_conv_bc_bias: float32 [256], replicated
- grad_a_log: float32 [32], P('tensor')
- grad_dt_bias: float32 [32], P('tensor')
- grad_d_skip: float32 [32], P('tensor')
- grad_gate_gain: float32 [2048], P('tensor')
- grad_w_out: float32 [2048, 1024], P('tensor', 'dp')
All inputs are finite; a program needn't handle non-finite values.
Results may differ from a plain program's by a relative error of at most 0.019.
Values may be sent and summed in bfloat16 or wider, within the bound.
A program may use at most 320 MiB of HBM per device.

v0:
```python
import jax
import jax.numpy as jnp
from jax import lax
from jax.sharding import PartitionSpec as P

BLOCK = 256
LENGTH = 1024


epsilon = 1e-05
highest = lax.Precision.HIGHEST


def depthwise(signal, kernel, offset):
    tap_count = kernel.shape[0]
    length_now = signal.shape[1]
    padded = jnp.pad(signal, ((0, 0), (tap_count - 1, 0), (0, 0)))
    running = jnp.zeros_like(signal) + offset
    for tap_index in range(tap_count):
        running = running + kernel[tap_index] * padded[:, tap_index : tap_index + length_now, :]
    return running


def spanned_scan(heads_in, keys_in, queries_in, step_size, rates):
    seq_count = heads_in.shape[0]
    head_count = heads_in.shape[2]
    head_width = heads_in.shape[3]
    causal = jnp.arange(BLOCK)[:, None] >= jnp.arange(BLOCK)[None, :]
    carried = jnp.zeros((seq_count, head_count, head_width, keys_in.shape[-1]), jnp.float32)
    results = []
    for block_index in range(LENGTH // BLOCK):
        lower = block_index * BLOCK
        input_block = heads_in[:, lower : lower + BLOCK]
        key_block = keys_in[:, lower : lower + BLOCK]
        query_block = queries_in[:, lower : lower + BLOCK]
        step_block = jnp.swapaxes(step_size[:, lower : lower + BLOCK], 1, 2)
        rate_block = jnp.swapaxes(rates[:, lower : lower + BLOCK], 1, 2)
        cumulative = jnp.cumsum(rate_block, axis=2)
        gap_rates = cumulative[:, :, :, None] - cumulative[:, :, None, :]
        decays = jnp.exp(jnp.where(causal[None, None, :, :], gap_rates, -jnp.inf))
        intersection = jnp.einsum("stn,sun->stu", query_block, key_block, precision=highest)
        weights = intersection[:, None, :, :] * decays * step_block[:, :, None, :]
        inside = jnp.einsum("shtu,suhp->sthp", weights, input_block, precision=highest)
        before = jnp.einsum("stn,shpn->sthp", query_block, carried, precision=highest)
        before = before * jnp.swapaxes(jnp.exp(cumulative), 1, 2)[..., None]
        remaining = jnp.exp(cumulative[:, :, -1:] - cumulative) * step_block
        fresh = jnp.einsum(
            "shu,suhp,sun->shpn", remaining, input_block, key_block, precision=highest
        )
        carried = carried * jnp.exp(cumulative[:, :, -1])[:, :, None, None] + fresh
        results.append(inside + before)
    return jnp.concatenate(results, axis=1)


def on_device(
    hidden_in,
    norm_gain,
    w_zx,
    w_dt,
    w_bc,
    conv_x,
    conv_x_bias,
    conv_bc,
    conv_bc_bias,
    a_log,
    dt_bias,
    d_skip,
    gate_gain,
    w_out,
    cotangent,
):
    model_width = hidden_in.shape[1]
    head_count = a_log.shape[0]
    inner_local = gate_gain.shape[0]
    inner_total = inner_local * lax.axis_size("tensor")
    state_width = w_bc.shape[1] // 2
    flat_zx = w_zx.reshape(model_width, 2 * inner_local)
    residual_in = hidden_in.astype(jnp.float32)
    inverse = lax.rsqrt(jnp.mean(residual_in * residual_in, axis=-1, keepdims=True) + epsilon)
    normed = (residual_in * inverse * norm_gain).astype(jnp.bfloat16)
    gathered = lax.all_gather(normed, "tensor", axis=0, tiled=True)
    group_rows = gathered.shape[0]
    seq_count = group_rows // LENGTH
    projected = jnp.dot(gathered, flat_zx, preferred_element_type=jnp.float32)
    gate_pre = projected[:, :inner_local]
    conv_in = projected[:, inner_local:]
    state_in = jnp.dot(gathered, w_bc, preferred_element_type=jnp.float32)
    step_raw = jnp.dot(gathered, w_dt, preferred_element_type=jnp.float32)

    def shaped(values):
        return values.reshape(seq_count, LENGTH, -1)

    def local_mixer(
        conv_part,
        state_part,
        gate_part,
        step_part,
        kernel_x,
        offset_x,
        kernel_bc,
        offset_bc,
        log_rate,
        step_offset,
        skip_gain,
    ):
        mixed_in = jax.nn.silu(depthwise(shaped(conv_part), kernel_x, offset_x))
        state_mix = jax.nn.silu(depthwise(shaped(state_part), kernel_bc, offset_bc))
        step_size = jax.nn.softplus(shaped(step_part) + step_offset)
        rates = step_size * -jnp.exp(log_rate)
        heads_in = mixed_in.reshape(seq_count, LENGTH, head_count, -1)
        scanned = spanned_scan(
            heads_in, state_mix[..., :state_width], state_mix[..., state_width:], step_size, rates
        )
        scanned = scanned + skip_gain[:, None] * heads_in
        gated_in = scanned.reshape(seq_count, LENGTH, -1) * jax.nn.silu(shaped(gate_part))
        return gated_in.reshape(group_rows, -1)

    gated_in, pullback = jax.vjp(
        local_mixer,
        conv_in,
        state_in,
        gate_pre,
        step_raw,
        conv_x,
        conv_x_bias,
        conv_bc,
        conv_bc_bias,
        a_log,
        dt_bias,
        d_skip,
    )
    square_sum = lax.psum(jnp.sum(gated_in * gated_in, axis=-1), "tensor")
    inverse_two = lax.rsqrt(square_sum / inner_total + epsilon)[:, None]
    normed_two = (gated_in * inverse_two * gate_gain).astype(jnp.bfloat16)
    mixed = lax.psum_scatter(
        jnp.dot(normed_two, w_out, preferred_element_type=jnp.float32).astype(jnp.bfloat16),
        "tensor",
        scatter_dimension=0,
        tiled=True,
    ).astype(jnp.float32)
    output = (residual_in + mixed).astype(jnp.bfloat16)
    cot_rows = lax.all_gather(cotangent, "tensor", axis=0, tiled=True)
    grad_w_out = jnp.einsum("rc,rd->cd", normed_two, cot_rows, preferred_element_type=jnp.float32)
    grad_normed_two = jnp.einsum("rd,cd->rc", cot_rows, w_out, preferred_element_type=jnp.float32)
    grad_gate_gain = jnp.sum(grad_normed_two * gated_in * inverse_two, axis=0)
    scaled = grad_normed_two * gate_gain
    cross = lax.psum(jnp.sum(scaled * gated_in, axis=-1), "tensor")
    grad_gated = inverse_two * scaled - gated_in * inverse_two**3 * (cross / inner_total)[:, None]
    (
        grad_conv_in,
        grad_state_part,
        grad_gate_pre,
        grad_step_raw,
        grad_conv_x,
        grad_conv_x_bias,
        grad_conv_bc,
        grad_conv_bc_bias,
        grad_a_log,
        grad_dt_bias,
        grad_d_skip,
    ) = pullback(grad_gated)
    state_rows = lax.psum_scatter(
        grad_state_part.astype(jnp.bfloat16), "tensor", scatter_dimension=0, tiled=True
    )
    proj_low = jnp.concatenate([grad_gate_pre, grad_conv_in], axis=-1).astype(jnp.bfloat16)
    step_low = grad_step_raw.astype(jnp.bfloat16)
    step_part = step_low
    first = jnp.einsum("rk,dk->rd", proj_low, flat_zx, preferred_element_type=jnp.float32)
    grad_normed = lax.psum_scatter(
        (
            first + jnp.einsum("rh,dh->rd", step_part, w_dt, preferred_element_type=jnp.float32)
        ).astype(jnp.bfloat16),
        "tensor",
        scatter_dimension=0,
        tiled=True,
    ).astype(jnp.float32)
    grad_normed = grad_normed + jnp.einsum(
        "rk,dk->rd", state_rows, w_bc, preferred_element_type=jnp.float32
    )
    grad_norm_gain = jnp.sum(grad_normed * residual_in * inverse, axis=0)
    weighted = grad_normed * norm_gain
    grad_input = inverse * weighted - residual_in * inverse**3 * jnp.mean(
        weighted * residual_in, axis=-1, keepdims=True
    )
    input_grad = (grad_input + cotangent.astype(jnp.float32)).astype(jnp.bfloat16)
    grad_w_zx = jnp.einsum("rd,rk->dk", gathered, proj_low, preferred_element_type=jnp.float32)
    grad_w_zx = grad_w_zx.reshape(model_width, 2, inner_local)
    grad_w_dt = jnp.einsum("rd,rh->dh", gathered, step_low, preferred_element_type=jnp.float32)
    grad_w_bc = jnp.einsum("rd,rk->dk", normed, state_rows, preferred_element_type=jnp.float32)
    grad_w_zx, grad_w_dt, grad_w_out, grad_w_bc = (
        lax.psum_scatter(
            grad_w_zx.astype(jnp.bfloat16), "dp", scatter_dimension=0, tiled=True
        ).astype(jnp.float32),
        lax.psum_scatter(
            grad_w_dt.astype(jnp.bfloat16), "dp", scatter_dimension=0, tiled=True
        ).astype(jnp.float32),
        lax.psum_scatter(
            grad_w_out.astype(jnp.bfloat16), "dp", scatter_dimension=1, tiled=True
        ).astype(jnp.float32),
        lax.psum_scatter(
            grad_w_bc.astype(jnp.bfloat16), "dp", scatter_dimension=0, tiled=True
        ).astype(jnp.float32),
    )
    grad_conv_x, grad_conv_x_bias, grad_a_log, grad_dt_bias, grad_d_skip, grad_gate_gain = lax.psum(
        (grad_conv_x, grad_conv_x_bias, grad_a_log, grad_dt_bias, grad_d_skip, grad_gate_gain), "dp"
    )
    grad_norm_gain, grad_conv_bc, grad_conv_bc_bias = lax.psum(
        (grad_norm_gain, grad_conv_bc, grad_conv_bc_bias), ("dp", "tensor")
    )
    grad_w_bc = lax.psum(grad_w_bc.astype(jnp.bfloat16), "tensor").astype(jnp.float32)
    return (
        output,
        input_grad,
        grad_norm_gain,
        grad_w_zx,
        grad_w_dt,
        grad_w_bc,
        grad_conv_x,
        grad_conv_x_bias,
        grad_conv_bc,
        grad_conv_bc_bias,
        grad_a_log,
        grad_dt_bias,
        grad_d_skip,
        grad_gate_gain,
        grad_w_out,
    )


def solution(mesh):
    in_specs = (
        P(("dp", "tensor"), None),
        P(),
        P(None, None, "tensor"),
        P(None, "tensor"),
        P(),
        P(None, "tensor"),
        P("tensor"),
        P(),
        P(),
        P("tensor"),
        P("tensor"),
        P("tensor"),
        P("tensor"),
        P("tensor", None),
        P(("dp", "tensor"), None),
    )
    out_specs = (
        P(("dp", "tensor"), None),
        P(("dp", "tensor"), None),
        P(),
        P("dp", None, "tensor"),
        P("dp", "tensor"),
        P("dp", None),
        P(None, "tensor"),
        P("tensor"),
        P(),
        P(),
        P("tensor"),
        P("tensor"),
        P("tensor"),
        P("tensor"),
        P("tensor", "dp"),
    )
    return jax.shard_map(
        on_device, mesh=mesh, in_specs=in_specs, out_specs=out_specs, check_vma=False
    )
```

profile of v0, /device:TPU:0, one launch (start us, length us, event | category | flops | bytes accessed | tf_op | source)
XLA Modules:
  0.0 1371.5 jit_solution(11869868064644947780)
XLA Ops:
  18.4 148.3 %all-gather.3.cloned.1.call-done = bf16[4096,1024]{1,0:T(8,128)(2,1)} async-done(((bf16[1024,1024]{1,0:T(8,128)(2,1)}), bf16[4096,1024]{1,0:T(8,128)(2,1)}) %all-gather.3.cloned.1.call-update) | async-done | bytes 8388624 | tf_op jit(solution)/shard_map/all_gather | solution.py:81
  220.1 12.2 fusion.373
  243.1 13.1 reshape.533
  256.2 12.8 copy.409
  269.1 19.0 %fusion.38 = (f32[4,1024,512]{2,1,0:T(8,128)}, f32[4,1024,512]{2,1,0:T(8,128)}) fusion(f32[4,1024,512]{2,1,0:T(8,128)} %bitcast.424, f32[512]{0:T(512)S(1)} %bitcast.472, f32[512]{0:T(512)S(1)} %bitcast.474, f32[512]{0:T(512)S(1)} %bitcast.470, f32[512]{0:T(512)S(1)} %bitcast.468, f32[512]{0:T(512)S(1)} %copy-done.116), kind=kLoop, calls=%fused_computation.74 | loop fusion | flops 25165824 | bytes 25176064 | tf_op jit(solution)/shard_map/jvp(jit(silu))/mul | solution.py:106
  315.6 10.8 bitcast_add_fusion.5
  339.7 12.5 bitcast_add_fusion.4
  366.4 12.5 bitcast_add_fusion.3
  387.4 12.5 bitcast_add_fusion.6
  402.8 12.8 multiply_reduce_fusion.13
  415.6 15.9 %psum.84 = f32[4096]{0:T(1024)S(1)} all-reduce(f32[4096]{0:T(1024)S(1)} %bitcast.467), channel_id=1, replica_groups=mesh['dp'=8,'tensor'=4] {'tensor'}, use_global_device_ids=true, to_apply=%region_10.11 | all-reduce | flops 4096 | bytes 32768 | tf_op jit(solution)/shard_map/psum | solution.py:132
  431.5 12.0 fusion.12
  443.5 16.0 %psum.85 = f32[4096]{0:T(1024)S(1)} all-reduce(f32[4096]{0:T(1024)S(1)} %get-tuple-element.16), channel_id=1, replica_groups=mesh['dp'=8,'tensor'=4] {'tensor'}, use_global_device_ids=true, to_apply=%region_13.14 | all-reduce | flops 4096 | bytes 32768 | tf_op jit(solution)/shard_map/psum | solution.py:147
  459.5 12.1 fusion.9
  471.6 12.9 reshape.527
  484.5 12.8 copy.410
  651.6 29.4 %fusion.42 = (f32[4,8,256]{2,1,0:T(8,128)S(1)}, f32[4,8,256]{2,1,0:T(8,128)S(1)}, f32[4,8,256]{2,1,0:T(8,128)}, f32[4,256,256]{2,1,0:T(8,128)S(1)}, f32[4,256,25...) fusion(f32[4,8,256]{2,1,0:T(8,128)S(1)} %copy-done.74, ...), kind=kOutput, calls=%fused_computation.86 | convolution fusion | flops 1718517760 | bytes 38600704 | tf_op jit(solution)/shard_map/transpose(jvp(shtu,suhp->sthp))/dot_general | solution.py:43
  768.3 11.1 fusion.364
  806.7 34.8 %multiply_reduce_fusion = (f32[512]{0:T(512)S(1)}, f32[512]{0:T(512)S(1)}, f32[512]{0:T(512)S(1)}, f32[512]{0:T(512)S(1)}, f32[512]{0:T(512)S(1)}, /*index=5*/f3...) fusion(f32[4096,512]{1,0:T(8,128)} %get-tuple-element.94, f32[4096,1024]{1,0:T(8,128)} %copy-done.6, ...), kind=kLoop, calls=%fused_computation.31 | loop fusion | flops 88077312 | bytes 79706112 | tf_op jit(solution)/shard_map/transpose(jvp())/reduce_sum | solution.py:114
  852.2 13.6 broadcast_multiply_fusion
  865.9 13.2 fusion.5
  879.1 12.8 fusion.155
  896.0 10.4 convolution_convert_fusion.1
  908.8 14.8 %fusion.40 = f32[4096,1024]{1,0:T(8,128)} fusion(bf16[1024,1024]{1,0:T(8,128)(2,1)S(1)} %bitcast.443, bf16[4096,512]{1,0:T(8,128)(2,1)} %bitcast.433, bf16[4096,512]{1,0:T(8,128)(2,1)} %bitcast.430), kind=kOutput, calls=%fused_computation.84 | convolution fusion | flops 8606711808 | bytes 27262976 | tf_op jit(solution)/shard_map/rk,dk->rd/dot_general | solution.py:168
  923.7 11.5 add_convert_fusion
  946.4 24.7 %all-reduce.48 = (f32[4,512]{1,0:T(4,128)}, f32[512]{0:T(512)}, f32[8]{0:T(128)}, f32[8]{0:T(128)}, f32[8]{0:T(128)}, /*index=5*/f32[512]{0:T(512)}) all-reduce(f32[4,512]{1,0:T(4,128)S(1)} %pad_add_fusion.10, f32[512]{0:T(512)S(1)} %get-tuple-element.38, f32[8]{0:T(128)S(1)} %negate_multiply_fusion, ...), channel_id=1, replica_groups=mesh['dp'=8,'tensor'=4] {'dp'}, use_global_device_ids=true, to_apply=%region_61.62 | all-reduce | flops 3096 | bytes 24768 | tf_op jit(solution)/shard_map/psum | solution.py:204
  972.6 16.2 %all-reduce.54.cloned.1.call-done = bf16[1024,2,512]{2,1,0:T(2,128)(2,1)} async-done(((bf16[1024,2,512]{2,1,0:T(2,128)(2,1)}), bf16[1024,2,512]{2,1,0:T(2,128)(2,1)}) %all-reduce.54.cloned.1.call-update) | async-done | bytes 2097168
  990.7 36.9 %reduce-scatter.21.cloned.1.call-done = bf16[128,512]{1,0:T(8,128)(2,1)} async-done(((bf16[1024,512]{1,0:T(8,128)(2,1)}), bf16[128,512]{1,0:T(8,128)(2,1)}) %reduce-scatter.21.cloned.1.call-update) | async-done | bytes 131088
  1029.3 34.7 %all-reduce.52.cloned.1.call-done = bf16[128,256]{1,0:T(8,128)(2,1)} async-done(((bf16[128,256]{1,0:T(8,128)(2,1)}), bf16[128,256]{1,0:T(8,128)(2,1)}) %all-reduce.52.cloned.1.call-update) | async-done | bytes 65552 | tf_op jit(solution)/shard_map/psum | solution.py:210
  1065.5 145.1 %reduce-scatter.13.cloned.1.call-done = bf16[1024,1024]{1,0:T(8,128)(2,1)} async-done(((bf16[4096,1024]{1,0:T(8,128)(2,1)}), bf16[1024,1024]{1,0:T(8,128)(2,1)}) %reduce-scatter.13.cloned.1.call-update) | async-done | bytes 2097168 | tf_op jit(solution)/shard_map/reduce_scatter | solution.py:169
  1216.0 44.9 %all-reduce.47 = (f32[1024]{0:T(1024)}, f32[4,256]{1,0:T(4,128)}, f32[256]{0:T(256)}) all-reduce(f32[1024]{0:T(1024)S(1)} %get-tuple-element.52, f32[4,256]{1,0:T(4,128)S(1)} %pad_add_fusion.11, f32[256]{0:T(256)S(1)} %get-tuple-element.54), channel_id=1, replica_groups=mesh['dp'=8,'tensor'=4] {'dp','tensor'}, use_global_device_ids=true, to_apply=%region_52.53 | all-reduce | flops 2304 | bytes 18432 | tf_op jit(solution)/shard_map/psum | solution.py:207
  1260.9 98.1 %reduce-scatter.11.cloned.1.call-done = bf16[1024,1024]{1,0:T(8,128)(2,1)} async-done(((bf16[4096,1024]{1,0:T(8,128)(2,1)}), bf16[1024,1024]{1,0:T(8,128)(2,1)}) %reduce-scatter.11.cloned.1.call-update) | async-done | bytes 2097168 | tf_op jit(solution)/shard_map/reduce_scatter | solution.py:135
  (496 shorter events, 454.8 us)
Async XLA Ops:
  7.2 424.3 %copy-start = (bf16[512,1024]{1,0:T(8,128)(2,1)S(1)}, bf16[512,1024]{1,0:T(8,128)(2,1)}, u32[]{:S(2)}) copy-start(bf16[512,1024]{1,0:T(8,128)(2,1)} %param.28) | copy-start | bytes 3145732
  7.2 159.5 %all-gather.3.cloned.1.call-start = ((), (), s32[]{:S(2)}) async-start(), calls=%async_computation.6 | async-start | bytes 10485760 | tf_op jit(solution)/shard_map/all_gather | solution.py:81
  14.2 152.5 %copy-start.59 = (bf16[1024,8]{0,1:T(8,128)(2,1)S(1)}, bf16[1024,8]{0,1:T(8,128)(2,1)}, u32[]{:S(2)}) copy-start(bf16[1024,8]{0,1:T(8,128)(2,1)} %param.18) | copy-start | bytes 49156
  14.2 417.2 %all-gather.5.cloned.1.call-start = ((), (), s32[]{:S(2)}) async-start(), calls=%async_computation.8 | async-start | bytes 10485760 | tf_op jit(solution)/shard_map/all_gather | solution.py:142
  15.0 833.9 %reduce-scatter.15.cloned.1.call-start = ((), (), s32[]{:S(2)}) async-start(), calls=%async_computation.10 | async-start | bytes 2621440 | tf_op jit(solution)/shard_map/reduce_scatter | solution.py:162
  15.1 324.5 %copy-start.55 = (pred[256,256]{1,0:T(8,128)(4,1)}, pred[256,256]{1,0:T(8,128)(4,1)S(1)}, u32[]{:S(2)}) copy-start(pred[256,256]{1,0:T(8,128)(4,1)S(1)} %iota_compare_fusion) | copy-start | bytes 196612
  15.1 159.5 %copy-start.123 = (f32[8]{0:T(128)}, f32[8]{0:T(128)S(1)}, u32[]{:S(2)}) copy-start(f32[8]{0:T(128)S(1)} %exponential_negate_fusion) | copy-start | bytes 100
  15.3 387.5 %copy-start.87 = (f32[512]{0:T(512)}, f32[512]{0:T(512)S(1)}, u32[]{:S(2)}) copy-start(f32[512]{0:T(512)S(1)} %mul.782) | copy-start | bytes 6148
  16.5 252.6 %copy-start.89 = (f32[1,512]{1,0:T(1,128)}, f32[1,512]{1,0:T(1,128)S(1)}, u32[]{:S(2)}) copy-start(f32[1,512]{1,0:T(1,128)S(1)} %get-tuple-element.131) | copy-start | bytes 6148
  16.5 252.6 %copy-start.91 = (f32[1,512]{1,0:T(1,128)}, f32[1,512]{1,0:T(1,128)S(1)}, u32[]{:S(2)}) copy-start(f32[1,512]{1,0:T(1,128)S(1)} %get-tuple-element.132) | copy-start | bytes 6148
  16.5 252.6 %copy-start.93 = (f32[1,512]{1,0:T(1,128)}, f32[1,512]{1,0:T(1,128)S(1)}, u32[]{:S(2)}) copy-start(f32[1,512]{1,0:T(1,128)S(1)} %get-tuple-element.133) | copy-start | bytes 6148
  18.4 156.2 %copy-start.121 = (f32[8]{0:T(128)S(1)}, f32[8]{0:T(128)}, u32[]{:S(2)}) copy-start(f32[8]{0:T(128)} %param.25) | copy-start | bytes 100
  179.0 30.2 %copy-start.7 = (f32[4,1024,8]{2,0,1:T(4,128)}, f32[4,1024,8]{2,0,1:T(4,128)S(1)}, u32[]{:S(2)}) copy-start(f32[4,1024,8]{2,0,1:T(4,128)S(1)} %get-tuple-element.106) | copy-start | bytes 393220
  196.1 119.5 %copy-start.49 = (f32[4,8,256]{2,1,0:T(8,128)}, f32[4,8,256]{2,1,0:T(8,128)S(1)}, u32[]{:S(2)}) copy-start(f32[4,8,256]{2,1,0:T(8,128)S(1)} %add_bitcast_fusion.6) | copy-start | bytes 98308
  199.8 139.8 %copy-start.51 = (f32[4,8,256]{2,1,0:T(8,128)}, f32[4,8,256]{2,1,0:T(8,128)S(1)}, u32[]{:S(2)}) copy-start(f32[4,8,256]{2,1,0:T(8,128)S(1)} %add_bitcast_fusion.5) | copy-start | bytes 98308
  220.1 167.2 %copy-start.53 = (f32[4,256,8]{1,2,0:T(8,128)}, f32[4,256,8]{1,2,0:T(8,128)S(1)}, u32[]{:S(2)}) copy-start(f32[4,256,8]{1,2,0:T(8,128)S(1)} %copy.376) | copy-start | bytes 98308
  505.0 95.5 %copy-start.1 = (f32[4,1024,8,64]{1,3,2,0:T(8,128)}, f32[4,1024,8,64]{1,3,2,0:T(8,128)S(1)}, u32[]{:S(2)}) copy-start(f32[4,1024,8,64]{1,3,2,0:T(8,128)S(1)} %multiply_multiply_fusion) | copy-start | bytes 25165828
  651.5 29.4 %copy-start.5 = (f32[4,1024,256]{2,1,0:T(8,128)S(1)}, f32[4,1024,256]{2,1,0:T(8,128)}, u32[]{:S(2)}) copy-start(f32[4,1024,256]{2,1,0:T(8,128)} %copy-done.3) | copy-start | bytes 12582916
  651.6 32.1 %copy-start.27 = (f32[4,256,128]{2,1,0:T(8,128)S(1)}, f32[4,256,128]{2,1,0:T(8,128)}, u32[]{:S(2)}) copy-start(f32[4,256,128]{2,1,0:T(8,128)} %fusion.235) | copy-start | bytes 1572868
  736.6 31.7 %copy-start.122 = (f32[8]{0:T(128)S(1)}, f32[8]{0:T(128)}, u32[]{:S(2)}) copy-start(f32[8]{0:T(128)} %param.25) | copy-start | bytes 100
  736.6 31.7 %copy-start.124 = (f32[8]{0:T(128)S(1)}, f32[8]{0:T(128)}, u32[]{:S(2)}) copy-start(f32[8]{0:T(128)} %copy-done.123) | copy-start | bytes 100
  806.7 117.0 %reduce-scatter.17.cloned.1.call-start = ((), (), s32[]{:S(2)}) async-start(), calls=%async_computation.11 | async-start | bytes 589824 | tf_op jit(solution)/shard_map/reduce_scatter | solution.py:200
  852.1 119.0 %reduce-scatter.19.cloned.1.call-start = ((), (), s32[]{:S(2)}) async-start(), calls=%async_computation.13 | async-start | bytes 294912
  865.8 122.9 %all-reduce.54.cloned.1.call-start = ((), (), s32[]{:S(2)}) async-start(), calls=%async_computation.15 | async-start | bytes 4194304
  896.0 131.6 %reduce-scatter.21.cloned.1.call-start = ((), (), s32[]{:S(2)}) async-start(), calls=%async_computation.14 | async-start | bytes 1179648
  908.8 155.2 %all-reduce.52.cloned.1.call-start = ((), (), s32[]{:S(2)}) async-start(), calls=%async_computation.12 | async-start | bytes 131072 | tf_op jit(solution)/shard_map/psum | solution.py:210
  923.7 286.9 %reduce-scatter.13.cloned.1.call-start = ((), (), s32[]{:S(2)}) async-start(), calls=%async_computation.9 | async-start | bytes 10485760 | tf_op jit(solution)/shard_map/reduce_scatter | solution.py:169
  935.2 423.7 %reduce-scatter.11.cloned.1.call-start = ((), (), s32[]{:S(2)}) async-start(), calls=%async_computation.7 | async-start | bytes 10485760 | tf_op jit(solution)/shard_map/reduce_scatter | solution.py:135
  944.3 266.2 %copy-start.11 = (bf16[1024,1024]{1,0:T(8,128)(2,1)S(1)}, bf16[1024,1024]{1,0:T(8,128)(2,1)}, u32[]{:S(2)}) copy-start(bf16[1024,1024]{1,0:T(8,128)(2,1)} %param.15) | copy-start | bytes 6291460
  944.3 266.2 %copy-start.62 = (f32[1024]{0:T(1024)S(1)}, f32[1024]{0:T(1024)}, u32[]{:S(2)}) copy-start(f32[1024]{0:T(1024)} %copy-done.61) | copy-start | bytes 12292
  944.3 266.2 %copy-start.99 = (f32[1024]{0:T(1024)S(1)}, f32[1024]{0:T(1024)}, u32[]{:S(2)}) copy-start(f32[1024]{0:T(1024)} %param.16) | copy-start | bytes 12292
  1065.5 293.4 %copy-start.97 = (f32[1024]{0:T(1024)S(1)}, f32[1024]{0:T(1024)}, u32[]{:S(2)}) copy-start(f32[1024]{0:T(1024)} %get-tuple-element.135) | copy-start | bytes 12292
  (110 other events, 1115.0 us)
Sparse Core Ops, SparseCore 0:
  14.4 152.3 all-gather.2
  168.3 147.8 all-gather.4
  806.8 42.0 reduce-scatter.14
  852.7 33.4 reduce-scatter.16
  889.6 33.5 reduce-scatter.18
  927.2 61.4 all-reduce.53
  992.3 35.2 reduce-scatter.20
  1030.0 33.9 all-reduce.51
  1066.3 144.1 reduce-scatter.12
  1212.7 146.1 reduce-scatter.10
where the time goes:
time: 1380 us; the launch traced here: 1370 us
  waiting for transfers between devices  487 us (35%)
  matrix products  341 us (25%)
  other arithmetic  251 us (18%)
  local copies, waits for them, and re-layouts  174 us (13%)
  blocking collectives  101 us (7%)
  between operations  16.4 us (1%)
    all_gather x1, waiting for transfers between devices, on_device(): gathered = lax.all_gather(normed, 'tensor', axis=0, tiled=True)  148 us
    reduce_scatter x1, waiting for transfers between devices, on_device(): lax.psum_scatter((first + jnp.einsum('rh,dh->rd', step_part, w_dt, prefer...  145 us
    dot_general x12, matrix products, spanned_scan(): jnp.einsum('shtu,suhp->sthp', weights, input_block, precision=highest)  141 us
    reduce_scatter x1, waiting for transfers between devices, on_device(): lax.psum_scatter(jnp.dot(normed_two, w_out, preferred_element_type=jnp.fl...  98.1 us
    another operation x26, other arithmetic  70.1 us
    unnamed x13, waiting for transfers between devices  53.9 us
    psum x1, blocking collectives, on_device(): lax.psum((grad_norm_gain, grad_conv_bc, grad_conv_bc_bias), ('dp', 'tenso...  44.9 us
    dot_general x11, matrix products, spanned_scan(): jnp.einsum('stn,shpn->sthp', query_block, carried, precision=highest)  35.7 us
  transfers between devices with their start and end apart: 10, of which 7 were waited for; matrix products, arithmetic and copies ran while one was open for 28% of the time, Pallas kernels for 0%

commit v1 on v0

--- a/solution.py
+++ b/solution.py
@@ -1,6 +1,8 @@
 import jax
 import jax.numpy as jnp
 from jax import lax
+from jax.experimental import pallas as pl
+from jax.experimental.pallas import tpu as pltpu
 from jax.sharding import PartitionSpec as P
 
 BLOCK = 256
@@ -227,6 +229,474 @@
     )
 
 
+f32 = jnp.float32
+bf16 = jnp.bfloat16
+BLOCKS = LENGTH // BLOCK
+LANES = 128
+
+
+def silu_parts(values):
+    gate = 1.0 / (1.0 + jnp.exp(-values))
+    return values * gate, gate
+
+
+def delayed(values, steps):
+    if steps == 0:
+        return values
+    moved = pltpu.roll(values, steps, 0)
+    position = lax.broadcasted_iota(jnp.int32, values.shape, 0)
+    return jnp.where(position >= steps, moved, 0.0)
+
+
+def advanced(values, steps):
+    if steps == 0:
+        return values
+    length = values.shape[0]
+    moved = pltpu.roll(values, length - steps, 0)
+    position = lax.broadcasted_iota(jnp.int32, values.shape, 0)
+    return jnp.where(position < length - steps, moved, 0.0)
+
+
+def contract(left, right, left_dim, right_dim):
+    return lax.dot_general(
+        left, right, (((left_dim,), (right_dim,)), ((), ())), preferred_element_type=f32
+    )
+
+
+def causal_mask():
+    later = lax.broadcasted_iota(jnp.int32, (BLOCK, BLOCK), 0)
+    earlier = lax.broadcasted_iota(jnp.int32, (BLOCK, BLOCK), 1)
+    return later >= earlier
+
+
+def fill_products(keys, queries, products):
+    for block in range(BLOCKS):
+        rows = slice(block * BLOCK, (block + 1) * BLOCK)
+        product = contract(queries[rows, :], keys[rows, :], 1, 1)
+        products[block] = jnp.where(causal_mask(), product, 0.0)
+
+
+def convolved(values, par):
+    total = par[4:5, :] + par[3:4, :] * values
+    for tap in range(3):
+        total = total + par[tap : tap + 1, :] * delayed(values, 3 - tap)
+    return total
+
+
+def block_parts(block, col_ref, left):
+    rows = slice(block * BLOCK, (block + 1) * BLOCK)
+    col = col_ref[0, rows, :]
+    cum = jnp.where(left, col[:, 0:1], col[:, 1:2])
+    step = jnp.where(left, col[:, 2:3], col[:, 3:4])
+    return rows, col, cum, step
+
+
+def forward_kernel(z_ref, x_ref, b_ref, c_ref, par_ref, row_ref, col_ref,
+                   g_ref, y_ref, st_ref, products):
+    @pl.when(pl.program_id(0) == 0)
+    def _():
+        fill_products(b_ref, c_ref, products)
+
+    par = par_ref[...]
+    xs, _ = silu_parts(convolved(x_ref[...], par))
+    left = lax.broadcasted_iota(jnp.int32, (BLOCK, LANES), 1) < LANES // 2
+    state = jnp.zeros((LANES, LANES), f32)
+    for block in range(BLOCKS):
+        rows, col, cum, step = block_parts(block, col_ref, left)
+        keys, queries = b_ref[rows, :], c_ref[rows, :]
+        last = cum[BLOCK - 1 : BLOCK, :]
+        stepped = xs[rows, :] * step
+        stepped_low = stepped.astype(bf16)
+        sides = []
+        for side in range(2):
+            gap = col[:, side : side + 1] - row_ref[0, side : side + 1, rows]
+            weights = products[block] * jnp.exp(jnp.minimum(gap, 0.0))
+            sides.append(contract(weights.astype(bf16), stepped_low, 1, 0))
+        scanned = jnp.where(left, sides[0], sides[1])
+        scanned = scanned + jnp.exp(cum) * contract(queries, state.astype(bf16), 1, 0)
+        y_ref[rows, :] = scanned
+        st_ref[0, block] = state
+        gate, _ = silu_parts(z_ref[rows, :])
+        g_ref[rows, :] = (scanned + par[5:6, :] * xs[rows, :]) * gate
+        if block < BLOCKS - 1:
+            fresh = contract(keys, (stepped * jnp.exp(last - cum)).astype(bf16), 0, 0)
+            state = state * jnp.exp(last) + fresh
+
+
+def backward_kernel(z_ref, x_ref, b_ref, c_ref, par_ref, row_ref, col_ref, y_ref, st_ref,
+                    dyn_ref, rc_ref, dz_ref, dx_ref, pc_ref, small_ref, db_ref, dc_ref,
+                    products, grad_products, dconv_ref):
+    pair = pl.program_id(0)
+
+    @pl.when(pair == 0)
+    def _():
+        fill_products(b_ref, c_ref, products)
+        grad_products[...] = jnp.zeros_like(grad_products)
+        db_ref[...] = jnp.zeros_like(db_ref)
+        dc_ref[...] = jnp.zeros_like(dc_ref)
+
+    par = par_ref[...]
+    before = x_ref[...]
+    conv = convolved(before, par)
+    xs, conv_gate = silu_parts(conv)
+    conv_slope = conv_gate * (1.0 + conv * (1.0 - conv_gate))
+    left = lax.broadcasted_iota(jnp.int32, (BLOCK, LANES), 1) < LANES // 2
+    row_at = lax.broadcasted_iota(jnp.int32, (BLOCK, LANES), 0)
+    grad_state = jnp.zeros((LANES, LANES), f32)
+    gain_sum = jnp.zeros((1, LANES), f32)
+    skip_sum = jnp.zeros((1, LANES), f32)
+    for block in reversed(range(BLOCKS)):
+        rows, col, cum, step = block_parts(block, col_ref, left)
+        keys, queries = b_ref[rows, :], c_ref[rows, :]
+        last = cum[BLOCK - 1 : BLOCK, :]
+        inputs = xs[rows, :]
+        scanned = y_ref[rows, :]
+        z = z_ref[rows, :]
+        gate, gate_sig = silu_parts(z)
+        full = scanned + par[5:6, :] * inputs
+        gated = full * gate
+        dyn = dyn_ref[rows, :]
+        inverse, coef = rc_ref[rows, 0:1], rc_ref[rows, 1:2]
+        scaled = dyn * inverse
+        gain_sum = gain_sum + jnp.sum(scaled * gated, axis=0, keepdims=True)
+        dg = scaled * par[6:7, :] - gated * coef
+        dz = dg * full * (gate_sig * (1.0 + z * (1.0 - gate_sig)))
+        dz_ref[rows, :] = dz.astype(bf16)
+        dy = dg * gate
+        skip_sum = skip_sum + jnp.sum(dy * inputs, axis=0, keepdims=True)
+        stepped = inputs * step
+        stepped_low = stepped.astype(bf16)
+        dy_low = dy.astype(bf16)
+        sides = []
+        total = grad_products[block]
+        for side in range(2):
+            gap = col[:, side : side + 1] - row_ref[0, side : side + 1, rows]
+            decay = jnp.exp(jnp.minimum(gap, 0.0))
+            weights = (products[block] * decay).astype(bf16)
+            sides.append(contract(weights, dy_low, 0, 0))
+            own = left if side == 0 else jnp.logical_not(left)
+            dy_own = jnp.where(own, dy, 0.0).astype(bf16)
+            total = total + decay * contract(dy_own, stepped_low, 1, 1)
+        grad_products[block] = total
+        grown = jnp.exp(cum)
+        decayed = jnp.exp(last - cum)
+        state = st_ref[0, block]
+        dy_grown = (grown * dy).astype(bf16)
+        dc_ref[rows, :] += contract(dy_grown, state.astype(bf16), 1, 1)
+        grad_state_low = grad_state.astype(bf16)
+        late = decayed * contract(keys, grad_state_low, 1, 0)
+        db_ref[rows, :] += contract((decayed * stepped).astype(bf16), grad_state_low, 1, 1)
+        kept = jnp.where(left, sides[0], sides[1]) + late
+        stepped_round = stepped_low.astype(f32)
+        at_end = jnp.sum(stepped_round * late, axis=0, keepdims=True)
+        at_end = at_end + jnp.exp(last) * jnp.sum(state * grad_state, axis=0, keepdims=True)
+        dcum = dy_low.astype(f32) * scanned - stepped_round * kept
+        dcum = dcum + jnp.where(row_at == BLOCK - 1, at_end, 0.0)
+        dstep = inputs * kept
+        sums = [
+            jnp.sum(jnp.where(own, part, 0.0), axis=1, keepdims=True)
+            for part in (dcum, dstep)
+            for own in (left, jnp.logical_not(left))
+        ]
+        for place, column in enumerate(sums):
+            pc_ref[0, rows, place : place + 1] = column
+        dxs = par[5:6, :] * dy + step * kept
+        dconv_ref[rows, :] = dxs * conv_slope[rows, :]
+        if block > 0:
+            grad_state = grad_state * jnp.exp(last) + contract(queries, dy_grown, 0, 0)
+    dconv = dconv_ref[...]
+    dx = par[3:4, :] * dconv
+    small_ref[3:4, :] = jnp.sum(dconv * before, axis=0, keepdims=True)
+    for tap in range(3):
+        dx = dx + par[tap : tap + 1, :] * advanced(dconv, 3 - tap)
+        moved = delayed(before, 3 - tap)
+        small_ref[tap : tap + 1, :] = jnp.sum(dconv * moved, axis=0, keepdims=True)
+    dx_ref[...] = dx.astype(bf16)
+    small_ref[4:5, :] = jnp.sum(dconv, axis=0, keepdims=True)
+    small_ref[5:6, :] = skip_sum
+    small_ref[6:7, :] = gain_sum
+    small_ref[7:8, :] = jnp.zeros_like(gain_sum)
+
+    @pl.when(pair == pl.num_programs(0) - 1)
+    def _():
+        for block in range(BLOCKS):
+            rows = slice(block * BLOCK, (block + 1) * BLOCK)
+            grad = jnp.where(causal_mask(), grad_products[block], 0.0).astype(bf16)
+            dc_ref[rows, :] += contract(grad, b_ref[rows, :], 1, 0)
+            db_ref[rows, :] += contract(grad, c_ref[rows, :], 0, 0)
+
+
+def lanes_of(first):
+    return pl.BlockSpec((LENGTH, LANES), lambda pair: (0, first + pair))
+
+
+def fixed(shape):
+    return pl.BlockSpec(shape, lambda pair: (0,) * len(shape))
+
+
+def per_pair(*shape):
+    return pl.BlockSpec((1,) + shape, lambda pair: (pair,) + (0,) * len(shape))
+
+
+def scan_specs(pairs):
+    return [
+        lanes_of(0),
+        lanes_of(pairs),
+        fixed((LENGTH, LANES)),
+        fixed((LENGTH, LANES)),
+        pl.BlockSpec((8, LANES), lambda pair: (0, pair)),
+        per_pair(2, LENGTH),
+        per_pair(LENGTH, 4),
+    ]
+
+
+def forward_scan(pairs, projected, keys, queries, par, rows, cols):
+    width = pairs * LANES
+    return pl.pallas_call(
+        forward_kernel,
+        grid=(pairs,),
+        in_specs=scan_specs(pairs),
+        out_specs=[lanes_of(0), lanes_of(0), per_pair(BLOCKS, LANES, LANES)],
+        out_shape=[
+            jax.ShapeDtypeStruct((LENGTH, width), f32),
+            jax.ShapeDtypeStruct((LENGTH, width), f32),
+            jax.ShapeDtypeStruct((pairs, BLOCKS, LANES, LANES), f32),
+        ],
+        scratch_shapes=[pltpu.VMEM((BLOCKS, BLOCK, BLOCK), f32)],
+        compiler_params=pltpu.CompilerParams(vmem_limit_bytes=44 * 2**20),
+        name="forward_scan",
+    )(projected, projected, keys, queries, par, rows, cols)
+
+
+def backward_scan(pairs, projected, keys, queries, par, rows, cols, scanned, states, dyn, rc):
+    width = pairs * LANES
+    return pl.pallas_call(
+        backward_kernel,
+        grid=(pairs,),
+        in_specs=scan_specs(pairs)
+        + [lanes_of(0), per_pair(BLOCKS, LANES, LANES), lanes_of(0), fixed((LENGTH, 2))],
+        out_specs=[
+            lanes_of(0),
+            lanes_of(0),
+            per_pair(LENGTH, 4),
+            pl.BlockSpec((8, LANES), lambda pair: (0, pair)),
+            fixed((LENGTH, LANES)),
+            fixed((LENGTH, LANES)),
+        ],
+        out_shape=[
+            jax.ShapeDtypeStruct((LENGTH, width), bf16),
+            jax.ShapeDtypeStruct((LENGTH, width), bf16),
+            jax.ShapeDtypeStruct((pairs, LENGTH, 4), f32),
+            jax.ShapeDtypeStruct((8, width), f32),
+            jax.ShapeDtypeStruct((LENGTH, LANES), f32),
+            jax.ShapeDtypeStruct((LENGTH, LANES), f32),
+        ],
+        scratch_shapes=[
+            pltpu.VMEM((BLOCKS, BLOCK, BLOCK), f32),
+            pltpu.VMEM((BLOCKS, BLOCK, BLOCK), f32),
+            pltpu.VMEM((LENGTH, LANES), f32),
+        ],
+        compiler_params=pltpu.CompilerParams(vmem_limit_bytes=44 * 2**20),
+        name="backward_scan",
+    )(projected, projected, keys, queries, par, rows, cols, scanned, states, dyn, rc)
+
+
+def on_device_sequence(
+    hidden_in,
+    norm_gain,
+    w_zx,
+    w_dt,
+    w_bc,
+    conv_x,
+    conv_x_bias,
+    conv_bc,
+    conv_bc_bias,
+    a_log,
+    dt_bias,
+    d_skip,
+    gate_gain,
+    w_out,
+    cotangent,
+):
+    model_width = hidden_in.shape[1]
+    data_size = lax.axis_size("dp")
+    group = lax.axis_size("tensor")
+    data_at = lax.axis_index("dp")
+    inner_local = gate_gain.shape[0]
+    inner = inner_local * group
+    heads_local = a_log.shape[0]
+    heads = heads_local * group
+    head_width = inner // heads
+    pairs = inner // LANES
+    share = model_width // data_size
+    out_share = inner_local // data_size
+    both = ("dp", "tensor")
+
+    mine = lax.dynamic_slice_in_dim(w_zx, data_at * share, share, axis=0)
+    weights_zx = lax.all_gather(mine, both, axis=0)
+    weights_zx = weights_zx.reshape(data_size, group, share, 2, inner_local)
+    weights_zx = weights_zx.transpose(0, 2, 3, 1, 4).reshape(model_width, 2 * inner)
+    mine = lax.dynamic_slice_in_dim(w_out, data_at * out_share, out_share, axis=0)
+    weights_out = lax.all_gather(mine, both, axis=0)
+    weights_out = weights_out.reshape(data_size, group, out_share, model_width)
+    weights_out = weights_out.transpose(1, 0, 2, 3).reshape(inner, model_width)
+    packed = jnp.concatenate(
+        [
+            conv_x,
+            conv_x_bias[None],
+            gate_gain[None],
+            jnp.pad(jnp.stack([a_log, dt_bias, d_skip]), ((0, 0), (0, inner_local - heads_local))),
+            w_dt.astype(f32).reshape(-1, inner_local),
+        ],
+        axis=0,
+    )
+    packed = lax.all_gather(packed, "tensor", axis=0)
+    wide = packed[:, :6].transpose(1, 0, 2).reshape(6, inner)
+    small = packed[:, 6:9, :heads_local].transpose(1, 0, 2).reshape(3, heads)
+    a_log_all, dt_bias_all, d_skip_all = small[0], small[1], small[2]
+    weights_dt = packed[:, 9:].reshape(group, model_width, heads_local)
+    weights_dt = weights_dt.transpose(1, 0, 2).reshape(model_width, heads).astype(bf16)
+
+    residual_in = hidden_in.astype(f32)
+    inverse = lax.rsqrt(jnp.mean(residual_in * residual_in, axis=-1, keepdims=True) + epsilon)
+    normed = (residual_in * inverse * norm_gain).astype(bf16)
+    state_in = jnp.dot(normed, w_bc, preferred_element_type=f32)
+
+    def state_mixer(values, kernel, offset):
+        return jax.nn.silu(depthwise(values[None], kernel, offset))[0]
+
+    state_mix, state_pullback = jax.vjp(state_mixer, state_in, conv_bc, conv_bc_bias)
+    state_low = state_mix.astype(bf16)
+    keys, queries = state_low[:, :LANES], state_low[:, LANES:]
+    projected = jnp.dot(normed, weights_zx, preferred_element_type=f32)
+    step_raw = jnp.dot(normed, weights_dt, preferred_element_type=f32) + dt_bias_all
+    step = jax.nn.softplus(step_raw)
+    decay_rate = -jnp.exp(a_log_all)
+    rates = (step * decay_rate).reshape(BLOCKS, BLOCK, heads)
+    lower = (jnp.arange(BLOCK)[:, None] >= jnp.arange(BLOCK)[None, :]).astype(f32)
+    cumulative = jnp.einsum("tu,buh->bth", lower, rates, precision=highest)
+    cumulative = cumulative.reshape(LENGTH, heads)
+    rows = cumulative.T.reshape(pairs, 2, LENGTH)
+    cols = jnp.concatenate(
+        [cumulative.reshape(LENGTH, pairs, 2), step.reshape(LENGTH, pairs, 2)], axis=-1
+    ).transpose(1, 0, 2)
+    par = jnp.concatenate(
+        [
+            wide[:5],
+            jnp.repeat(d_skip_all, head_width)[None],
+            wide[5:6],
+            jnp.zeros((1, inner), f32),
+        ],
+        axis=0,
+    )
+    gated, scanned, states = forward_scan(pairs, projected, keys, queries, par, rows, cols)
+    gain_all = wide[5]
+    inverse_two = lax.rsqrt(jnp.mean(gated * gated, axis=-1, keepdims=True) + epsilon)
+    normed_two = (gated * inverse_two * gain_all).astype(bf16)
+    output = (
+        residual_in + jnp.dot(normed_two, weights_out, preferred_element_type=f32)
+    ).astype(bf16)
+    grad_normed_two = jnp.einsum(
+        "rd,cd->rc", cotangent, weights_out, preferred_element_type=f32
+    )
+    grad_w_out = jnp.einsum(
+        "rc,rd->cd", normed_two, cotangent, preferred_element_type=f32
+    ).astype(bf16)
+    grad_w_out = grad_w_out.reshape(group, inner_local, data_size, model_width // data_size)
+    grad_w_out = grad_w_out.transpose(2, 0, 1, 3).reshape(
+        data_size, group * inner_local, model_width // data_size
+    )
+    grad_w_out = lax.psum_scatter(grad_w_out, "dp", scatter_dimension=0, tiled=True)[0]
+    grad_w_out = lax.psum_scatter(grad_w_out, "tensor", scatter_dimension=0, tiled=True)
+    grad_w_out = grad_w_out.astype(f32)
+    cross = jnp.sum(grad_normed_two * gain_all * gated, axis=-1, keepdims=True)
+    rc = jnp.concatenate([inverse_two, inverse_two**3 * cross / inner], axis=-1)
+    dz, dx, pieces, grads, grad_keys, grad_queries = backward_scan(
+        pairs, projected, keys, queries, par, rows, cols, scanned, states, grad_normed_two, rc
+    )
+    pieces = pieces.transpose(1, 0, 2)
+    grad_cum = pieces[:, :, :2].reshape(BLOCKS, BLOCK, heads)
+    grad_rate = jnp.einsum("tu,bth->buh", lower, grad_cum, precision=highest)
+    grad_rate = grad_rate.reshape(LENGTH, heads)
+    grad_step = pieces[:, :, 2:].reshape(LENGTH, heads) + grad_rate * decay_rate
+    grad_a_log = jnp.sum(grad_rate * step, axis=0) * decay_rate
+    grad_step = grad_step * jax.nn.sigmoid(step_raw)
+    grad_dt_bias = jnp.sum(grad_step, axis=0)
+    grad_d_skip = jnp.sum(grads[5].reshape(heads, head_width), axis=1)
+    grad_state_in, grad_conv_bc, grad_conv_bc_bias = state_pullback(
+        jnp.concatenate([grad_keys, grad_queries], axis=1)
+    )
+    dbc = grad_state_in.astype(bf16)
+    ddt = grad_step.astype(bf16)
+    proj_low = jnp.concatenate([dz, dx], axis=1)
+    grad_w_zx = jnp.einsum("rd,rk->dk", normed, proj_low, preferred_element_type=f32)
+    grad_w_zx = lax.psum_scatter(grad_w_zx.astype(bf16), "dp", scatter_dimension=0, tiled=True)
+    grad_w_zx = grad_w_zx.reshape(share, 2, group, inner_local).transpose(2, 0, 1, 3)
+    grad_w_zx = lax.psum_scatter(
+        grad_w_zx.reshape(group * share, 2 * inner_local),
+        "tensor",
+        scatter_dimension=0,
+        tiled=True,
+    )
+    grad_w_zx = grad_w_zx.astype(f32).reshape(share, 2, inner_local)
+    side = jnp.concatenate([dbc, ddt, jnp.zeros((LENGTH, LANES - heads), bf16)], axis=1)
+    grad_side = jnp.einsum("rd,rk->dk", normed, side, preferred_element_type=f32).astype(bf16)
+    grad_side = lax.psum_scatter(grad_side, "dp", scatter_dimension=0, tiled=True)
+    grad_side = lax.psum(grad_side, "tensor").astype(f32)
+    bc_width = w_bc.shape[1]
+    grad_w_bc = grad_side[:, :bc_width]
+    tensor_at = lax.axis_index("tensor")
+    grad_w_dt = lax.dynamic_slice_in_dim(
+        grad_side, bc_width + tensor_at * heads_local, heads_local, axis=1
+    )
+    grad_normed = jnp.einsum("rk,dk->rd", proj_low, weights_zx, preferred_element_type=f32)
+    grad_normed = grad_normed + jnp.einsum("rk,dk->rd", dbc, w_bc, preferred_element_type=f32)
+    grad_normed = grad_normed + jnp.einsum(
+        "rh,dh->rd", ddt, weights_dt, preferred_element_type=f32
+    )
+    grad_norm_gain = jnp.sum(grad_normed * residual_in * inverse, axis=0)
+    weighted = grad_normed * norm_gain
+    grad_input = inverse * weighted - residual_in * inverse**3 * jnp.mean(
+        weighted * residual_in, axis=-1, keepdims=True
+    )
+    input_grad = (grad_input + cotangent.astype(f32)).astype(bf16)
+    sizes = []
+    flat = []
+    for piece in (
+        grads[:7], grad_norm_gain, grad_conv_bc, grad_conv_bc_bias,
+        grad_a_log, grad_dt_bias, grad_d_skip,
+    ):
+        flat.append(piece.reshape(-1))
+        sizes.append(flat[-1].shape[0])
+    flat = jnp.concatenate(flat)
+    flat = jnp.pad(flat, (0, -flat.shape[0] % 1024)).reshape(-1, LANES)
+    flat = lax.psum(flat, both).reshape(-1)
+    starts = [sum(sizes[:at]) for at in range(len(sizes))]
+    parts = [flat[start : start + size] for start, size in zip(starts, sizes)]
+
+    def own(values, width):
+        return lax.dynamic_slice_in_dim(values, tensor_at * width, width, axis=-1)
+
+    wide_sums = own(parts[0].reshape(7, inner), inner_local)
+    return (
+        output,
+        input_grad,
+        parts[1],
+        grad_w_zx,
+        grad_w_dt,
+        grad_w_bc,
+        wide_sums[:4],
+        wide_sums[4],
+        parts[2].reshape(conv_bc.shape),
+        parts[3],
+        own(parts[4], heads_local),
+        own(parts[5], heads_local),
+        own(parts[6], heads_local),
+        wide_sums[6],
+        grad_w_out,
+    )
+
+
 def solution(mesh):
     in_specs = (
         P(("dp", "tensor"), None),
@@ -262,6 +732,15 @@
         P("tensor"),
         P("tensor", "dp"),
     )
-    return jax.shard_map(
-        on_device, mesh=mesh, in_specs=in_specs, out_specs=out_specs, check_vma=False
-    )
+
+    def program(*arrays):
+        whole_sequence = arrays[0].shape[0] // mesh.size == LENGTH
+        return jax.shard_map(
+            on_device_sequence if whole_sequence else on_device,
+            mesh=mesh,
+            in_specs=in_specs,
+            out_specs=out_specs,
+            check_vma=False,
+        )(*arrays)
+
+    return program

time: 1380 us -> 723 us (0.52)
  matrix products: 341 us -> 85.5 us
  other arithmetic: 251 us -> 30.4 us
  waiting for transfers between devices: 487 us -> 384 us
  Pallas kernels: 0 us -> 99.3 us
  local copies, waits for them, and re-layouts: 174 us -> 87.8 us
  blocking collectives: 101 us -> 16.3 us
    dot_general x56 -> x13, matrix products: 341 us -> 85.5 us  [the longest x1 16.3 us: on_device_sequence(): projected = jnp.dot(normed, weights_zx, preferred_element_type=f32)]
    psum x1 -> x2, waiting for transfers between devices: 34.7 us -> 140 us  [the longest x1 109 us: on_device_sequence(): flat = lax.psum(flat, both).reshape(-1)]
    psum x4 -> x0, blocking collectives: 101 us -> none  [the longest x1 44.9 us: on_device(): lax.psum((grad_norm_gain, grad_conv_bc, grad_conv_bc_bias), ('dp', 'tenso...]
    pallas_call x0 -> x2, Pallas kernels: none -> 99.3 us  [the longest x1 70.2 us: backward_scan(): pl.pallas_call(backward_kernel, grid=(pairs,), in_specs=scan_specs(pairs)...]
    reduce_scatter x4 -> x5, waiting for transfers between devices: 250 us -> 152 us  [the longest x1 70.2 us: on_device_sequence(): lax.psum_scatter(grad_w_zx.astype(bf16), 'dp', scatter_dimension=0, tiled...]
    another operation x26 -> x1, other arithmetic: 70.1 us -> 0.7 us  [on_device_sequence(): jnp.stack([a_log, dt_bias, d_skip])]
    reduce_sum x7 -> x3, other arithmetic: 70.7 us -> 3.33 us  [the longest x1 2.22 us: on_device_sequence(): grad_dt_bias = jnp.sum(grad_step, axis=0)]
    all_gather x2, waiting for transfers between devices: 148 us -> 90.7 us  [the longest x1 74.6 us: on_device_sequence(): weights_zx = lax.all_gather(mine, both, axis=0)]
  transfers between devices with their start and end apart: 10 -> 9, of which waited for: 7 -> 8; matrix products, arithmetic and copies ran while one was open for 28% -> 17% of each run, Pallas kernels for 0% -> 0%
where the time goes in v1:
time: 723 us; the launch traced here: 718 us
  waiting for transfers between devices  384 us (53%)
  Pallas kernels  99.3 us (14%)
  local copies, waits for them, and re-layouts  87.8 us (12%)
  matrix products  85.5 us (12%)
  other arithmetic  30.4 us (4%)
  blocking collectives  16.3 us (2%)
  between operations  14.6 us (2%)
    psum x1, waiting for transfers between devices, on_device_sequence(): flat = lax.psum(flat, both).reshape(-1)  109 us
    all_gather x1, waiting for transfers between devices, on_device_sequence(): weights_zx = lax.all_gather(mine, both, axis=0)  74.6 us
    reduce_scatter x1, waiting for transfers between devices, on_device_sequence(): lax.psum_scatter(grad_w_zx.astype(bf16), 'dp', scatter_dimension=0, tiled...  70.2 us
    pallas_call x1, Pallas kernels, backward_scan(): pl.pallas_call(backward_kernel, grid=(pairs,), in_specs=scan_specs(pairs)...  70.2 us
    reduce_scatter x1, waiting for transfers between devices, on_device_sequence(): lax.psum_scatter(grad_w_out, 'dp', scatter_dimension=0, tiled=True)[0]  35.4 us
    psum x1, waiting for transfers between devices, on_device_sequence(): grad_side = lax.psum(grad_side, 'tensor').astype(f32)  31 us
    pallas_call x1, Pallas kernels, forward_scan(): pl.pallas_call(forward_kernel, grid=(pairs,), in_specs=scan_specs(pairs),...  29.2 us
    reduce_scatter x1, waiting for transfers between devices, on_device_sequence(): lax.psum_scatter(grad_w_zx.reshape(group * share, 2 * inner_local), 'tens...  26.3 us
  transfers between devices with their start and end apart: 9, of which 8 were waited for; matrix products, arithmetic and copies ran while one was open for 17% of the time, Pallas kernels for 0%

profile of v1, /device:TPU:0, one launch (start us, length us, event | category | flops | bytes accessed | tf_op | source)
XLA Modules:
  0.0 717.8 jit_solution(5610172539625615319)
XLA Ops:
  13.0 16.3 %all-gather.3 = f32[4,25,512]{2,1,0:T(8,128)S(1)} all-gather(f32[1,25,512]{2,1,0:T(8,128)S(1)} %bitcast.160), channel_id=3, replica_groups=mesh['dp'=8,'tensor'=4] {'tensor'}, dimensions={0}, use_global_device_ids=true | all-gather | bytes 256000 | tf_op jit(solution)/shard_map/all_gather | solution.py:553
  35.2 5.2 copy.138
  40.4 4.7 copy.139
  45.3 2.4 fusion.48
  49.3 11.2 %maximum_bitcast_fusion.col_ref = f32[16,1024,4]{2,1,0:T(8,128)} fusion(f32[1024,16,2]{2,0,1:T(8,128)} %copy.139, f32[1024,16,2]{2,0,1:T(8,128)} %copy.138), kind=kLoop, calls=%fused_computation.10 | loop fusion | flops 65536 | bytes 524288 | tf_op jit(solution)/shard_map/transpose | solution.py:582
  60.6 16.1 %all-gather.9.cloned.1.call-done = bf16[2048,1024]{1,0:T(8,128)(2,1)} async-done(((bf16[64,1024]{1,0:T(8,128)(2,1)}), bf16[2048,1024]{1,0:T(8,128)(2,1)}) %all-gather.9.cloned.1.call-update) | async-done | bytes 4194320 | tf_op jit(solution)/shard_map/all_gather | solution.py:540
  76.7 4.9 copy.140
  81.6 74.6 %all-gather.7.cloned.1.call-done = bf16[4096,2,512]{2,1,0:T(2,128)(2,1)} async-done(((bf16[128,2,512]{2,1,0:T(2,128)(2,1)}), bf16[4096,2,512]{2,1,0:T(2,128)(2,1)}) %all-gather.7.cloned.1.call-update) | async-done | bytes 8388624 | tf_op jit(solution)/shard_map/all_gather | solution.py:536
  156.2 14.5 %copy.129 = bf16[8,4,128,2,512]{2,0,4,1,3:T(8,128)(2,1)} copy(bf16[8,4,128,2,512]{4,3,2,1,0:T(2,128)(2,1)} %bitcast.147) | data formatting | bytes 16777216 | tf_op jit(solution)/shard_map/reshape | solution.py:537
  170.7 16.3 %fusion.2.z_ref.x_ref = f32[1024,4096]{1,0:T(8,128)} fusion(bf16[512,8,8,128]{3,2,1,0:T(8,128)(2,1)} %bitcast.145, bf16[1024,1024]{1,0:T(8,128)(2,1)} %param.15, f32[1024]{0:T(1024)S(1)} %copy-done.19, f32[1024]{0:T(1024)S(1)} %get-tuple-element.159), kind=kOutput, calls=%fused_computation.8 | convolution fusion | flops 8594128896 | bytes 27271168 | tf_op jit(solution)/shard_map/dot_general | solution.py:571
  187.0 29.2 %forward_scan.1 = (f32[1024,2048]{1,0:T(8,128)}, f32[1024,2048]{1,0:T(8,128)}, f32[16,4,128,128]{3,2,1,0:T(8,128)S(1)}) custom-call(f32[1024,4096]{1,0:T(8,128)} %fusion.2.z_ref.x_ref, f32[1024,4096]{1,0:T(8,128)} %fusion.2.z_ref.x_ref, bf16[1024,128]{1,0:T(8,128)(2,1)S(1)} %get-tuple-element.150.b_ref, bf16[1024,128]{1,0:T(8,128)(2,1)S(1)} %get-tuple-element.149.c_ref, ...), custom_call_target="tpu_custom_call" | custom-call | tf_op jit(solution)/shard_map/forward_scan/pallas_call | solution.py:455
  216.2 10.8 %multiply_reduce_fusion = (f32[1024]{0:T(1024)S(1)}, f32[1024]{0:T(1024)S(1)}, f32[1024,2048]{1,0:T(8,128)}) fusion(f32[1024,2048]{1,0:T(8,128)} %get-tuple-element.24, f32[2048]{0:T(1024)S(1)} %bitcast.165, bf16[2048,1024]{1,0:T(8,128)(2,1)S(1)} %bitcast.149, bf16[1024,1024]{1,0:T(8,128)(2,1)S(1)} %copy-done.12), kind=kOutput, calls=%fused_computation.11 | convolution fusion | flops 4305451008 | bytes 23085056 | tf_op jit(solution)/shard_map/rd,cd->rc/dot_general | solution.py:599
  227.3 70.2 %backward_scan.1 = (bf16[1024,2048]{1,0:T(8,128)(2,1)S(1)}, bf16[1024,2048]{1,0:T(8,128)(2,1)}, f32[16,1024,4]{2,1,0:T(8,128)}, f32[8,2048]{1,0:T(8,128)S(1)}, f...) custom-call(f32[1024,4096]{1,0:T(8,128)} %fusion.2.z_ref.x_ref, f32[1024,4096]{1,0:T(8,128)} %fusion.2.z_ref.x_ref, ...), custom_call_target="tpu_custom_call" | custom-call | tf_op jit(solution)/shard_map/backward_scan/pallas_call | solution.py:473
  301.1 2.3 copy-done.4
  303.4 7.1 fusion.54
  310.5 5.2 copy.144
  316.2 5.5 copy.143
  327.1 4.1 convolution_convert_fusion.1
  331.2 8.8 %convert_bitcast_fusion = bf16[256,8,8,128]{3,1,2,0:T(8,128)(2,1)S(1)} fusion(bf16[1024,1024]{1,0:T(8,128)(2,1)} %param.29, f32[1024,2048]{1,0:T(8,128)} %get-tuple-element.24, f32[2048]{0:T(1024)S(1)} %bitcast.166, f32[1024]{0:T(1024)S(1)} %add_rsqrt_fusion), kind=kOutput, calls=%fused_computation.30 | convolution fusion | flops 4303355904 | bytes 14692352 | tf_op jit(solution)/shard_map/rc,rd->cd/dot_general | solution.py:602
  341.4 3.0 copy.149
  344.5 2.7 constant_dynamic-update-slice_fusion.1
  348.2 3.2 copy-done.15
  351.5 12.1 %convolution_convert_fusion = bf16[1024,4096]{1,0:T(8,128)(2,1)} fusion(bf16[1024,4096]{1,0:T(8,128)(2,1)S(1)} %constant_dynamic-update-slice_fusion, bf16[1024,1024]{1,0:T(8,128)(2,1)S(1)} %copy-done.6, f32[1024]{0:T(1024)S(1)} %copy-done.19, f32[1024]{0:T(1024)S(1)} %get-tuple-element.159), kind=kOutput, calls=%fused_computation.14 | convolution fusion | flops 8598323200 | bytes 18882560 | tf_op jit(solution)/shard_map/rd,rk->dk/dot_general | solution.py:632
  366.6 15.9 %fusion.16 = (f32[1024]{0:T(1024)S(1)}, f32[1024]{0:T(1024)S(1)}, f32[1024,1024]{1,0:T(8,128)}) fusion(bf16[1024,1024]{1,0:T(8,128)(2,1)S(1)} %copy-done.7, f32[1024]{0:T(1024)S(1)} %get-tuple-element.159, f32[1024]{0:T(1024)S(1)} %copy-done.19, f32[1024,1024]{1,0:T(8,128)S(1)} %fusion.37, f32[1024,1024]{1,0:T(8,128)S(1)} %fusion.60, ...), kind=kOutput, calls=%fused_computation.28 | convolution fusion | flops 8599369728 | bytes 31473664 | tf_op jit(solution)/shard_map/rk,dk->rd/dot_general | solution.py:652
  384.1 35.4 %reduce-scatter.12.cloned.1.call-done = bf16[1,2048,128]{2,1,0:T(8,128)(2,1)} async-done(((bf16[8,2048,128]{2,1,0:T(8,128)(2,1)}), bf16[1,2048,128]{2,1,0:T(8,128)(2,1)}) %reduce-scatter.12.cloned.1.call-update) | async-done | bytes 524304 | tf_op jit(solution)/shard_map/reduce_scatter | solution.py:609
  419.6 4.7 fusion.13
  424.3 70.2 %reduce-scatter.6.cloned.1.call-done = bf16[128,4096]{1,0:T(8,128)(2,1)} async-done(((bf16[1024,4096]{1,0:T(8,128)(2,1)}), bf16[128,4096]{1,0:T(8,128)(2,1)}) %reduce-scatter.6.cloned.1.call-update) | async-done | bytes 1048592 | tf_op jit(solution)/shard_map/reduce_scatter | solution.py:633
  498.4 11.2 %fusion.9 = bf16[1024,1024]{1,0:T(8,128)(2,1)} fusion(bf16[1024,1024]{1,0:T(8,128)(2,1)} %param.15, bf16[2048,1024]{1,0:T(8,128)(2,1)} %bitcast.148, f32[1024,2048]{1,0:T(8,128)} %get-tuple-element.24, f32[2048]{0:T(1024)S(1)} %bitcast.167, f32[1024]{0:T(1024)S(1)} %add_rsqrt_fusion), kind=kOutput, calls=%fused_computation.21 | convolution fusion | flops 4304404480 | bytes 16789504 | tf_op jit(solution)/shard_map/dot_general | solution.py:597
  509.7 108.7 %all-reduce.14.cloned.1.call-done = f32[136,128]{1,0:T(8,128)} async-done(((f32[136,128]{1,0:T(8,128)}), f32[136,128]{1,0:T(8,128)}) %all-reduce.14.cloned.1.call-update) | async-done | bytes 69648 | tf_op jit(solution)/shard_map/psum | solution.py:673
  626.2 31.0 %all-reduce.16.cloned.1.call-done = bf16[128,384]{1,0:T(8,128)(2,1)} async-done(((bf16[128,384]{1,0:T(8,128)(2,1)}), bf16[128,384]{1,0:T(8,128)(2,1)}) %all-reduce.16.cloned.1.call-update) | async-done | bytes 98320 | tf_op jit(solution)/shard_map/psum | solution.py:645
  660.4 20.5 %reduce-scatter.14.cloned.1.call-done = bf16[512,128]{1,0:T(8,128)(2,1)} async-done(((bf16[2048,128]{1,0:T(8,128)(2,1)}), bf16[512,128]{1,0:T(8,128)(2,1)}) %reduce-scatter.14.cloned.1.call-update) | async-done | bytes 131088 | tf_op jit(solution)/shard_map/reduce_scatter | solution.py:610
  682.6 26.3 %reduce-scatter.8.cloned.1.call-done = bf16[128,1024]{1,0:T(8,128)(2,1)} async-done(((bf16[512,1024]{1,0:T(8,128)(2,1)}), bf16[128,1024]{1,0:T(8,128)(2,1)}) %reduce-scatter.8.cloned.1.call-update) | async-done | bytes 262160 | tf_op jit(solution)/shard_map/reduce_scatter | solution.py:635
  (156 shorter events, 49.0 us)
Async XLA Ops:
  7.2 25.1 %copy-start.19 = (f32[1024]{0:T(1024)S(1)}, f32[1024]{0:T(1024)}, u32[]{:S(2)}) copy-start(f32[1024]{0:T(1024)} %param.16) | copy-start | bytes 12292
  7.2 69.5 %all-gather.9.cloned.1.call-start = ((), (), s32[]{:S(2)}) async-start(), calls=%async_computation.13 | async-start | bytes 4325376 | tf_op jit(solution)/shard_map/all_gather | solution.py:540
  9.0 147.2 %all-gather.7.cloned.1.call-start = ((), (), s32[]{:S(2)}) async-start(), calls=%async_computation.12 | async-start | bytes 8650752 | tf_op jit(solution)/shard_map/all_gather | solution.py:536
  9.9 21.3 %copy-start.5 = (bf16[1024,1024]{1,0:T(8,128)(2,1)S(1)}, bf16[1024,1024]{1,0:T(8,128)(2,1)}, u32[]{:S(2)}) copy-start(bf16[1024,1024]{1,0:T(8,128)(2,1)} %param.15) | copy-start | bytes 6291460
  10.0 373.4 %reduce-scatter.10.cloned.1.call-start = ((), (), s32[]{:S(2)}) async-start(), calls=%async_computation.8 | async-start | bytes 884736 | tf_op jit(solution)/shard_map/reduce_scatter | solution.py:644
  29.4 293.5 %copy-start.24 = (f32[32]{0:T(128)}, f32[32]{0:T(128)S(1)}, u32[]{:S(2)}) copy-start(f32[32]{0:T(128)S(1)} %neg.24) | copy-start | bytes 388
  40.4 4.9 copy-start.21
  40.4 4.9 copy-start.16
  45.1 2.5 copy-start.26
  187.0 29.2 %copy-start.9 = (bf16[4,8,64,1024]{3,2,1,0:T(8,128)(2,1)S(1)}, bf16[4,8,64,1024]{3,2,1,0:T(8,128)(2,1)}, u32[]{:S(2)}) copy-start(bf16[4,8,64,1024]{3,2,1,0:T(8,128)(2,1)} %copy.140) | copy-start | bytes 12582916
  187.0 29.2 %copy-start.12 = (bf16[1024,1024]{1,0:T(8,128)(2,1)S(1)}, bf16[1024,1024]{1,0:T(8,128)(2,1)}, u32[]{:S(2)}) copy-start(bf16[1024,1024]{1,0:T(8,128)(2,1)} %param.29) | copy-start | bytes 6291460
  216.2 10.8 %copy-start.2 = (f32[16,4,128,128]{3,2,1,0:T(8,128)}, f32[16,4,128,128]{3,2,1,0:T(8,128)S(1)}, u32[]{:S(2)}) copy-start(f32[16,4,128,128]{3,2,1,0:T(8,128)S(1)} %get-tuple-element.26.st_ref) | copy-start | bytes 12582916
  227.3 70.2 %copy-start.8 = (f32[1,1024,256]{2,1,0:T(8,128)S(1)}, f32[1,1024,256]{2,1,0:T(8,128)}, u32[]{:S(2)}) copy-start(f32[1,1024,256]{2,1,0:T(8,128)} %get-tuple-element.139) | copy-start | bytes 3145732
  297.5 3.6 copy-start.3
  297.5 5.9 copy-start.4
  316.1 9.0 %copy-start.11 = (f32[1,1024,256]{2,1,0:T(8,128)S(1)}, f32[1,1024,256]{2,1,0:T(8,128)}, u32[]{:S(2)}) copy-start(f32[1,1024,256]{2,1,0:T(8,128)} %get-tuple-element.144) | copy-start | bytes 3145732
  327.1 4.1 copy-start.13
  331.2 88.3 %reduce-scatter.12.cloned.1.call-start = ((), (), s32[]{:S(2)}) async-start(), calls=%async_computation.10 | async-start | bytes 4718592 | tf_op jit(solution)/shard_map/reduce_scatter | solution.py:609
  344.4 150.1 %reduce-scatter.6.cloned.1.call-start = ((), (), s32[]{:S(2)}) async-start(), calls=%async_computation.6 | async-start | bytes 9437184 | tf_op jit(solution)/shard_map/reduce_scatter | solution.py:633
  344.5 3.5 copy-start.10
  347.9 3.6 copy-start.6
  348.2 3.3 copy-start.15
  363.6 254.8 %all-reduce.14.cloned.1.call-start = ((), (), s32[]{:S(2)}) async-start(), calls=%async_computation.5 | async-start | bytes 139264 | tf_op jit(solution)/shard_map/psum | solution.py:673
  366.6 16.0 %copy-start.20 = (f32[256]{0:T(256)S(1)}, f32[256]{0:T(256)}, u32[]{:S(2)}) copy-start(f32[256]{0:T(256)} %get-tuple-element.130) | copy-start | bytes 3076
  366.6 16.0 %copy-start.22 = (f32[32]{0:T(128)S(1)}, f32[32]{0:T(128)}, u32[]{:S(2)}) copy-start(f32[32]{0:T(128)} %reduce_sum.156) | copy-start | bytes 388
  366.6 16.0 %copy-start.23 = (f32[32]{0:T(128)S(1)}, f32[32]{0:T(128)}, u32[]{:S(2)}) copy-start(f32[32]{0:T(128)} %get-tuple-element.135) | copy-start | bytes 388
  366.6 16.0 %copy-start.27 = (f32[32]{0:T(128)S(1)}, f32[32]{0:T(128)}, u32[]{:S(2)}) copy-start(f32[32]{0:T(128)} %mul.296) | copy-start | bytes 388
  366.6 53.0 %copy-start.18 = (f32[1024]{0:T(1024)S(1)}, f32[1024]{0:T(1024)}, u32[]{:S(2)}) copy-start(f32[1024]{0:T(1024)} %get-tuple-element.158) | copy-start | bytes 12292
  383.3 274.0 %all-reduce.16.cloned.1.call-start = ((), (), s32[]{:S(2)}) async-start(), calls=%async_computation.9 | async-start | bytes 196608 | tf_op jit(solution)/shard_map/psum | solution.py:645
  384.0 296.9 %reduce-scatter.14.cloned.1.call-start = ((), (), s32[]{:S(2)}) async-start(), calls=%async_computation.11 | async-start | bytes 655360 | tf_op jit(solution)/shard_map/reduce_scatter | solution.py:610
  419.5 289.3 %reduce-scatter.8.cloned.1.call-start = ((), (), s32[]{:S(2)}) async-start(), calls=%async_computation.7 | async-start | bytes 1310720 | tf_op jit(solution)/shard_map/reduce_scatter | solution.py:635
  498.4 212.7 %copy-start.1 = (bf16[1024,2,512]{2,1,0:T(2,128)(2,1)S(1)}, bf16[1024,2,512]{2,1,0:T(2,128)(2,1)}, u32[]{:S(2)}) copy-start(bf16[1024,2,512]{2,1,0:T(2,128)(2,1)} %param.17) | copy-start | bytes 6291460
  (5 other events, 8.5 us)
Sparse Core Ops, SparseCore 0:
  11.6 65.0 all-gather.8
  80.2 75.9 all-gather.6
  331.3 33.5 reduce-scatter.9
  368.1 51.3 reduce-scatter.11
  423.2 71.2 reduce-scatter.5
  500.5 117.8 all-reduce.13
  620.7 36.5 all-reduce.15
  659.6 21.2 reduce-scatter.13
  683.3 25.4 reduce-scatter.7
